TPU v7x, 32 devices: a whole 2x2x4 slice. The times are simulated.
32 devices in a mesh: videos: 8 (over z, x), heads: 4 (over y, core).
Axes of the slice: x: 2, y: 2, z: 4, core: 2. Of those that a mesh axis runs over, the one named last changes fastest.
Arguments:
- frames: bfloat16 [8, 8, 328, 768], P('videos', None, 'heads'), may hold values from -6 to 6
- out_grad: bfloat16 [8, 8, 328, 768], P('videos', None, 'heads'), may hold values from -6 to 6
- frame_tokens: int32 [8], P('videos'), may hold values from 197 to 325, as said below
- frame_count: int32 [8], P('videos'), may hold values from 2 to 8, as said below
- msg_fc_w: bfloat16 [768, 768], P(None, 'heads'), may hold values from -0.21875 to 0.21875
- msg_fc_b: bfloat16 [768], P('heads'), may hold values from -2 to 2
- msg_norm_g: bfloat16 [768], replicated, may hold values from 0.5 to 1.5
- msg_norm_b: bfloat16 [768], replicated, may hold values from -2 to 2
- msg_qkv_w: bfloat16 [3, 768, 768], P(None, None, 'heads'), may hold values from -0.21875 to 0.21875
- msg_qkv_b: bfloat16 [2, 768], P(None, 'heads'), may hold values from -2 to 2
- msg_out_w: bfloat16 [768, 768], P('heads'), may hold values from -0.4375 to 0.4375
- msg_out_b: bfloat16 [768], replicated, may hold values from -2 to 2
- norm1_g: bfloat16 [768], replicated, may hold values from 0.5 to 1.5
- norm1_b: bfloat16 [768], replicated, may hold values from -2 to 2
- attn_qkv_w: bfloat16 [3, 768, 768], P(None, None, 'heads'), may hold values from -0.21875 to 0.21875
- attn_qkv_b: bfloat16 [2, 768], P(None, 'heads'), may hold values from -2 to 2
- attn_out_w: bfloat16 [768, 768], P('heads'), may hold values from -1.75 to 1.75
- attn_out_b: bfloat16 [768], replicated, may hold values from -2 to 2
- norm2_g: bfloat16 [768], replicated, may hold values from 0.5 to 1.5
- norm2_b: bfloat16 [768], replicated, may hold values from -2 to 2
- fc1_w: bfloat16 [768, 3072], P(None, 'heads'), may hold values from -0.21875 to 0.21875
- fc1_b: bfloat16 [3072], P('heads'), may hold values from -2 to 2
- fc2_w: bfloat16 [3072, 768], P('heads'), may hold values from -0.109375 to 0.109375
- fc2_b: bfloat16 [768], replicated, may hold values from -2 to 2
Outputs:
- mixed_out: bfloat16 [8, 8, 328, 768], P('videos', None, 'heads')
- frames_grad: float32 [8, 8, 328, 768], P('videos', None, 'heads')
- msg_fc_w_grad: float32 [768, 768], P(None, 'heads')
- msg_fc_b_grad: float32 [768], P('heads')
- msg_norm_g_grad: float32 [768], P('heads')
- msg_norm_b_grad: float32 [768], P('heads')
- msg_qkv_w_grad: float32 [3, 768, 768], P(None, None, 'heads')
- msg_qkv_b_grad: float32 [2, 768], P(None, 'heads')
- msg_out_w_grad: float32 [768, 768], P('heads')
- msg_out_b_grad: float32 [768], P('heads')
- norm1_g_grad: float32 [768], P('heads')
- norm1_b_grad: float32 [768], P('heads')
- attn_qkv_w_grad: float32 [3, 768, 768], P(None, None, 'heads')
- attn_qkv_b_grad: float32 [2, 768], P(None, 'heads')
- attn_out_w_grad: float32 [768, 768], P('heads')
- attn_out_b_grad: float32 [768], P('heads')
- norm2_g_grad: float32 [768], P('heads')
- norm2_b_grad: float32 [768], P('heads')
- fc1_w_grad: float32 [768, 3072], P(None, 'heads')
- fc1_b_grad: float32 [3072], P('heads')
- fc2_w_grad: float32 [3072, 768], P('heads')
- fc2_b_grad: float32 [768], P('heads')
Inputs may be any that keep to these rules, and one draw needn't show every extreme that they name: `frame_tokens`: each video has 197 or 325 tokens a frame, and some video has 325. `frame_count`: some video has 8.
All inputs are finite; a program needn't handle non-finite values.
Results may differ from a plain program's by a relative error of at most 0.025.
Values may be sent and summed in bfloat16 or wider, within the bound.
No kernel may reach another device: no remote copies, remote signals or barrier semaphores. Data moves between devices by JAX's collectives and lax.ppermute only.
A program may use at most 192 MiB of HBM per device.

v0:
```python
import jax
import jax.numpy as jnp
from jax import lax
from jax.sharding import PartitionSpec as P

HEAD_DIM = 64


epsilon = 1e-05


def norm_forward(value, gains, offset):
    average = jnp.mean(value, -1, keepdims=True)
    centered = value - average
    spread = jnp.mean(centered * centered, -1, keepdims=True)
    inverse = lax.rsqrt(spread + epsilon)
    unit = centered * inverse
    return (unit * gains.astype(jnp.float32) + offset.astype(jnp.float32), unit, inverse)


def norm_backward(gradient, unit, inverse, gains):
    scaled = gradient * gains.astype(jnp.float32)
    average = jnp.mean(scaled, -1, keepdims=True)
    second = jnp.mean(scaled * unit, -1, keepdims=True)
    return inverse * (scaled - average - unit * second)


def split_heads(tensors):
    return tuple(
        (
            tensor.reshape(tensor.shape[:-1] + (tensor.shape[-1] // HEAD_DIM, HEAD_DIM))
            for tensor in tensors
        )
    )


def project(normed, weight, biases):
    stacked = jnp.einsum("...d,cde->c...e", normed, weight, preferred_element_type=jnp.float32)
    return (
        (stacked[0] + biases[0]).astype(jnp.bfloat16),
        stacked[1].astype(jnp.bfloat16),
        (stacked[2] + biases[1]).astype(jnp.bfloat16),
    )


def attend_forward(queries, key_rows, values, keymask):
    scale_factor = HEAD_DIM ** (-0.5)
    scores = (
        jnp.einsum("bqhe,bkhe->bhqk", queries, key_rows, preferred_element_type=jnp.float32)
        * scale_factor
    )
    scores = jnp.where(keymask, scores, -1e30)
    largest = jnp.max(scores, -1, keepdims=True)
    exponent = jnp.exp(scores - largest)
    totals = jnp.sum(exponent, -1, keepdims=True)
    chances = exponent / totals
    output = jnp.einsum(
        "bhqk,bkhe->bqhe", chances.astype(jnp.bfloat16), values, preferred_element_type=jnp.float32
    )
    return (output.astype(jnp.bfloat16), largest + jnp.log(totals))


def attend_backward(queries, key_rows, values, keymask, log_total, grad_heads):
    scale_factor = HEAD_DIM ** (-0.5)
    scores = (
        jnp.einsum("bqhe,bkhe->bhqk", queries, key_rows, preferred_element_type=jnp.float32)
        * scale_factor
    )
    scores = jnp.where(keymask, scores, -1e30)
    chances = jnp.exp(scores - log_total)
    grad_chances = jnp.einsum(
        "bqhe,bkhe->bhqk", grad_heads, values, preferred_element_type=jnp.float32
    )
    deltas = jnp.sum(chances * grad_chances, -1, keepdims=True)
    grad_scores = (chances * (grad_chances - deltas)).astype(jnp.bfloat16)
    grad_query = (
        jnp.einsum("bhqk,bkhe->bqhe", grad_scores, key_rows, preferred_element_type=jnp.float32)
        * scale_factor
    ).astype(jnp.bfloat16)
    grad_key = (
        jnp.einsum("bhqk,bqhe->bkhe", grad_scores, queries, preferred_element_type=jnp.float32)
        * scale_factor
    ).astype(jnp.bfloat16)
    grad_value = jnp.einsum(
        "bhqk,bqhe->bkhe",
        chances.astype(jnp.bfloat16),
        grad_heads,
        preferred_element_type=jnp.float32,
    ).astype(jnp.bfloat16)
    return (grad_query, grad_key, grad_value)


def on_device(
    frames,
    out_grad,
    frame_tokens,
    frame_count,
    msg_fc_w,
    msg_fc_b,
    msg_norm_g,
    msg_norm_b,
    msg_qkv_w,
    msg_qkv_b,
    msg_out_w,
    msg_out_b,
    norm1_g,
    norm1_b,
    attn_qkv_w,
    attn_qkv_b,
    attn_out_w,
    attn_out_b,
    norm2_g,
    norm2_b,
    fc1_w,
    fc1_b,
    fc2_w,
    fc2_b,
):
    local_videos, frame_slots, own_rows, features = frames.shape
    groups = lax.axis_size("heads")
    group_index = lax.axis_index("heads")
    all_rows = own_rows * groups
    local_width = msg_fc_w.shape[1]
    places = jnp.arange(all_rows + 1)
    row_masks = (places[None, :] < frame_tokens[:, None]) | (places == all_rows)[None, :]
    frame_masks = (jnp.arange(frame_slots)[None, :] < frame_count[:, None])[:, None, None, :]
    gathered = lax.all_gather(frames, "heads", axis=2, tiled=True)
    leading = gathered[:, :, 0, :]
    fc_part = jnp.dot(leading, msg_fc_w, preferred_element_type=jnp.float32) + msg_fc_b
    message = lax.all_gather(fc_part, "heads", axis=2, tiled=True)
    msg_normed, msg_unit, msg_inverse = norm_forward(message, msg_norm_g, msg_norm_b)
    msg_in = msg_normed.astype(jnp.bfloat16)
    msg_query, msg_key, msg_value = split_heads(project(msg_in, msg_qkv_w, msg_qkv_b))
    msg_heads, msg_lse = attend_forward(msg_query, msg_key, msg_value, frame_masks)
    msg_flat = msg_heads.reshape(local_videos, frame_slots, local_width)
    msg_part = jnp.dot(msg_flat, msg_out_w, preferred_element_type=jnp.float32)
    carried = message + lax.psum(msg_part, "heads") + msg_out_b

    def frame_forward(element):
        rows, extra, row_mask = element
        joined = jnp.concatenate([rows.astype(jnp.float32), extra[:, None, :]], 1)
        normed = norm_forward(joined, norm1_g, norm1_b)[0].astype(jnp.bfloat16)
        queries, key_rows, values = split_heads(project(normed, attn_qkv_w, attn_qkv_b))
        output, log_total = attend_forward(queries, key_rows, values, row_mask[None, None, None, :])
        flat = output.reshape(frame_slots, all_rows + 1, local_width)[:, :all_rows]
        return (flat, log_total, jnp.dot(flat, attn_out_w, preferred_element_type=jnp.float32))

    attn_heads, attn_lse, attn_part = lax.map(frame_forward, (gathered, carried, row_masks))
    attn_rows = (
        lax.psum_scatter(
            attn_part.astype(jnp.bfloat16), "heads", scatter_dimension=2, tiled=True
        ).astype(jnp.float32)
        + attn_out_b
    )
    mixed_rows = frames.astype(jnp.float32) + attn_rows
    normed_two, unit_two, inverse_two = norm_forward(mixed_rows, norm2_g, norm2_b)
    mlp_in = lax.all_gather(normed_two.astype(jnp.bfloat16), "heads", axis=2, tiled=True)
    hidden = jnp.dot(mlp_in, fc1_w, preferred_element_type=jnp.float32) + fc1_b
    sigmoid_part = jax.nn.sigmoid(1.702 * hidden)
    active = (hidden * sigmoid_part).astype(jnp.bfloat16)
    mlp_part = jnp.dot(active, fc2_w, preferred_element_type=jnp.float32)
    mlp_rows = (
        lax.psum_scatter(
            mlp_part.astype(jnp.bfloat16), "heads", scatter_dimension=2, tiled=True
        ).astype(jnp.float32)
        + fc2_b
    )
    mixed_out = (mixed_rows + mlp_rows).astype(jnp.bfloat16)
    grad_top = out_grad.astype(jnp.float32)
    grad_full = lax.all_gather(out_grad, "heads", axis=2, tiled=True)
    fc2_w_grad = jnp.einsum("vfrk,vfrd->kd", active, grad_full, preferred_element_type=jnp.float32)
    grad_active = jnp.einsum("vfrd,kd->vfrk", grad_full, fc2_w, preferred_element_type=jnp.float32)
    grad_hidden = (
        grad_active * (sigmoid_part + 1.702 * hidden * sigmoid_part * (1.0 - sigmoid_part))
    ).astype(jnp.bfloat16)
    fc1_w_grad = jnp.einsum(
        "vfrd,vfrk->dk", mlp_in, grad_hidden, preferred_element_type=jnp.float32
    )
    fc1_b_grad = jnp.sum(grad_hidden.astype(jnp.float32), (0, 1, 2))
    norm_two_part = jnp.einsum(
        "vfrk,dk->vfrd", grad_hidden, fc1_w, preferred_element_type=jnp.float32
    )
    grad_normed_two = lax.psum_scatter(
        norm_two_part.astype(jnp.bfloat16), "heads", scatter_dimension=2, tiled=True
    ).astype(jnp.float32)
    grad_mixed = grad_top + norm_backward(grad_normed_two, unit_two, inverse_two, norm2_g)
    grad_attn = grad_mixed.astype(jnp.bfloat16)
    grad_attn_full = lax.all_gather(grad_attn, "heads", axis=2, tiled=True)

    def frame_backward(element):
        rows, extra, row_mask, heads_out, log_total, grad_rows = element
        joined = jnp.concatenate([rows.astype(jnp.float32), extra[:, None, :]], 1)
        normed, unit, inverse = norm_forward(joined, norm1_g, norm1_b)
        normed_low = normed.astype(jnp.bfloat16)
        queries, key_rows, values = split_heads(project(normed_low, attn_qkv_w, attn_qkv_b))
        heads_grad = jnp.einsum(
            "frd,ed->fre", grad_rows, attn_out_w, preferred_element_type=jnp.float32
        )
        heads_grad = jnp.concatenate([heads_grad, jnp.zeros_like(heads_grad[:, :1])], 1).astype(
            jnp.bfloat16
        )
        out_weight_grad = jnp.einsum(
            "fre,frd->ed", heads_out, grad_rows, preferred_element_type=jnp.float32
        )
        grad_query, grad_key, grad_value = attend_backward(
            queries,
            key_rows,
            values,
            row_mask[None, None, None, :],
            log_total,
            split_heads((heads_grad,))[0],
        )
        stacked = jnp.stack([grad_query, grad_key, grad_value]).reshape(
            (3,) + normed_low.shape[:-1] + (local_width,)
        )
        qkv_grad = jnp.einsum(
            "frd,cfre->cde", normed_low, stacked, preferred_element_type=jnp.float32
        )
        bias_grad = jnp.stack(
            [
                jnp.sum(stacked[0].astype(jnp.float32), (0, 1)),
                jnp.sum(stacked[2].astype(jnp.float32), (0, 1)),
            ]
        )
        grad_normed = jnp.einsum(
            "cfre,cde->frd", stacked, attn_qkv_w, preferred_element_type=jnp.float32
        )
        grad_joined = norm_backward(grad_normed, unit, inverse, norm1_g)
        gain_terms = jnp.stack([jnp.sum(grad_normed * unit, (0, 1)), jnp.sum(grad_normed, (0, 1))])
        return (grad_joined, out_weight_grad, qkv_grad, bias_grad, gain_terms)

    grad_joined, out_weight_grads, qkv_grads, bias_grads, gain_terms = lax.map(
        frame_backward, (gathered, carried, row_masks, attn_heads, attn_lse, grad_attn_full)
    )
    attn_out_w_grad = jnp.sum(out_weight_grads, 0)
    attn_qkv_w_grad = jnp.sum(qkv_grads, 0)
    attn_qkv_b_grad = jnp.sum(bias_grads, 0)
    norm_one_terms = jnp.sum(gain_terms, 0)
    grad_message = lax.psum(grad_joined[:, :, all_rows, :], "heads")
    grad_msg_low = grad_message.astype(jnp.bfloat16)
    msg_out_w_grad = jnp.einsum(
        "vfe,vfd->ed", msg_flat, grad_msg_low, preferred_element_type=jnp.float32
    )
    msg_heads_grad = jnp.einsum(
        "vfd,ed->vfe", grad_msg_low, msg_out_w, preferred_element_type=jnp.float32
    ).astype(jnp.bfloat16)
    msg_gq, msg_gk, msg_gv = attend_backward(
        msg_query, msg_key, msg_value, frame_masks, msg_lse, split_heads((msg_heads_grad,))[0]
    )
    msg_stacked = jnp.stack([msg_gq, msg_gk, msg_gv]).reshape(
        3, local_videos, frame_slots, local_width
    )
    msg_qkv_w_grad = jnp.einsum(
        "vfd,cvfe->cde", msg_in, msg_stacked, preferred_element_type=jnp.float32
    )
    msg_qkv_b_grad = jnp.stack(
        [
            jnp.sum(msg_stacked[0].astype(jnp.float32), (0, 1)),
            jnp.sum(msg_stacked[2].astype(jnp.float32), (0, 1)),
        ]
    )
    msg_norm_part = jnp.einsum(
        "cvfe,cde->vfd", msg_stacked, msg_qkv_w, preferred_element_type=jnp.float32
    )
    grad_msg_normed = lax.psum(msg_norm_part, "heads")
    grad_fc = grad_message + norm_backward(grad_msg_normed, msg_unit, msg_inverse, msg_norm_g)
    grad_fc_cols = lax.dynamic_slice_in_dim(
        grad_fc, group_index * local_width, local_width, 2
    ).astype(jnp.bfloat16)
    msg_fc_w_grad = jnp.einsum(
        "vfd,vfe->de", leading, grad_fc_cols, preferred_element_type=jnp.float32
    )
    msg_fc_b_grad = jnp.sum(grad_fc_cols.astype(jnp.float32), (0, 1))
    leading_grad = jnp.einsum(
        "vfe,de->vfd", grad_fc_cols, msg_fc_w, preferred_element_type=jnp.float32
    )
    frame_part = grad_joined[:, :, :all_rows, :].at[:, :, 0, :].add(leading_grad)
    single = (group_index == 0).astype(jnp.float32)
    small_stack = jnp.stack(
        [
            jnp.sum(grad_msg_normed * msg_unit, (0, 1)) * single,
            jnp.sum(grad_msg_normed, (0, 1)) * single,
            jnp.sum(grad_msg_low.astype(jnp.float32), (0, 1)) * single,
            norm_one_terms[0],
            norm_one_terms[1],
            jnp.sum(grad_attn.astype(jnp.float32), (0, 1, 2)),
            jnp.sum(grad_normed_two * unit_two, (0, 1, 2)),
            jnp.sum(grad_normed_two, (0, 1, 2)),
            jnp.sum(grad_top, (0, 1, 2)),
        ]
    )
    frame_grad, small_grads = (
        lax.psum_scatter(
            frame_part.astype(jnp.bfloat16), "heads", scatter_dimension=2, tiled=True
        ).astype(jnp.float32),
        lax.psum_scatter(
            small_stack.astype(jnp.bfloat16), "heads", scatter_dimension=1, tiled=True
        ).astype(jnp.float32),
    )
    frames_grad = grad_mixed + frame_grad
    totals = lax.psum(
        (
            msg_fc_w_grad,
            msg_fc_b_grad,
            msg_qkv_w_grad,
            msg_qkv_b_grad,
            msg_out_w_grad,
            attn_qkv_w_grad,
            attn_qkv_b_grad,
            attn_out_w_grad,
            fc1_w_grad,
            fc1_b_grad,
            fc2_w_grad,
            small_grads,
        ),
        "videos",
    )
    (
        msg_fc_w_grad,
        msg_fc_b_grad,
        msg_qkv_w_grad,
        msg_qkv_b_grad,
        msg_out_w_grad,
        attn_qkv_w_grad,
        attn_qkv_b_grad,
        attn_out_w_grad,
        fc1_w_grad,
        fc1_b_grad,
        fc2_w_grad,
        small_grads,
    ) = totals
    return (
        mixed_out,
        frames_grad,
        msg_fc_w_grad,
        msg_fc_b_grad,
        small_grads[0],
        small_grads[1],
        msg_qkv_w_grad,
        msg_qkv_b_grad,
        msg_out_w_grad,
        small_grads[2],
        small_grads[3],
        small_grads[4],
        attn_qkv_w_grad,
        attn_qkv_b_grad,
        attn_out_w_grad,
        small_grads[5],
        small_grads[6],
        small_grads[7],
        fc1_w_grad,
        fc1_b_grad,
        fc2_w_grad,
        small_grads[8],
    )


def solution(mesh):
    placed = (
        P("videos", None, "heads", None),
        P("videos", None, "heads", None),
        P("videos"),
        P("videos"),
        P(None, "heads"),
        P("heads"),
        P(),
        P(),
        P(None, None, "heads"),
        P(None, "heads"),
        P("heads", None),
        P(),
        P(),
        P(),
        P(None, None, "heads"),
        P(None, "heads"),
        P("heads", None),
        P(),
        P(),
        P(),
        P(None, "heads"),
        P("heads"),
        P("heads", None),
        P(),
    )
    return jax.shard_map(
        on_device,
        mesh=mesh,
        in_specs=placed,
        out_specs=(
            P("videos", None, "heads", None),
            P("videos", None, "heads", None),
            P(None, "heads"),
            P("heads"),
            P("heads"),
            P("heads"),
            P(None, None, "heads"),
            P(None, "heads"),
            P("heads", None),
            P("heads"),
            P("heads"),
            P("heads"),
            P(None, None, "heads"),
            P(None, "heads"),
            P("heads", None),
            P("heads"),
            P("heads"),
            P("heads"),
            P(None, "heads"),
            P("heads"),
            P("heads", None),
            P("heads"),
        ),
        check_vma=False,
    )
```

profile of v0, /device:TPU:0, one launch (start us, length us, event | category | flops | bytes accessed | tf_op | source)
XLA Modules:
  0.0 857.4 jit_solution(2907662959351658313)
XLA Ops:
  14.5 31.4 %all-gather.7.cloned.1.call-done = bf16[1,8,328,768]{3,1,0,2:T(8,128)(2,1)} async-done(((bf16[1,8,82,768]{3,1,0,2:T(8,128)(2,1)}), bf16[1,8,328,768]{3,1,0,2:T(8,128)(2,1)}) %all-gather.7.cloned.1.call-update) | async-done | bytes 4030480 | tf_op jit(solution)/shard_map/all_gather | solution.py:127
  47.0 5.3 all-gather.1
  58.0 10.4 %psum.105 = f32[1,8,768]{2,1,0:T(8,128)S(1)} all-reduce(f32[1,8,768]{2,1,0:T(8,128)S(1)} %convolution_bitcast_fusion.5), channel_id=1, replica_groups=mesh['videos'=8,'heads'=4] {'heads'}, use_global_device_ids=true, to_apply=%region_4.5 | all-reduce | flops 6144 | bytes 49152 | tf_op jit(solution)/shard_map/psum | solution.py:137
  101.8 44.1 %reduce-scatter.8.cloned.1.call-done = bf16[1,8,82,768]{3,1,2,0:T(8,128)(2,1)} async-done(((bf16[1,8,328,768]{3,1,2,0:T(8,128)(2,1)}), bf16[1,8,82,768]{3,1,2,0:T(8,128)(2,1)}) %reduce-scatter.8.cloned.1.call-update) | async-done | bytes 1007632 | tf_op jit(solution)/shard_map/reduce_scatter | solution.py:150
  151.6 33.1 %all-gather.9.cloned.1.call-done = bf16[1,8,328,768]{3,1,0,2:T(8,128)(2,1)} async-done(((bf16[1,8,82,768]{3,1,0,2:T(8,128)(2,1)}), bf16[1,8,328,768]{3,1,0,2:T(8,128)(2,1)}) %all-gather.9.cloned.1.call-update) | async-done | bytes 4030480 | tf_op jit(solution)/shard_map/all_gather | solution.py:157
  184.7 10.3 %multiply_convert_fusion.2 = (bf16[8,328,768]{2,1,0:T(8,128)(2,1)S(1)}, f32[8,328,768]{2,1,0:T(8,128)}) fusion(f32[768]{0:T(1024)S(1)} %convert_element_type.398, bf16[768,768]{1,0:T(8,128)(2,1)S(1)} %copy-done, bf16[1,8,328,768]{3,1,0,2:T(8,128)(2,1)} %all-gather.9.cloned.1.call-done), kind=kOutput, calls=%fused_computation.16 | convolution fusion | flops 3109502976 | bytes 17304576 | tf_op jit(solution)/shard_map/dot_general | solution.py:158
  197.0 6.1 convert_bitcast_fusion.1
  203.6 16.2 %all-gather.11.cloned.1.call-done = bf16[1,8,328,768]{3,1,0,2:T(8,128)(2,1)} async-done(((bf16[1,8,82,768]{3,1,0,2:T(8,128)(2,1)}), bf16[1,8,328,768]{3,1,0,2:T(8,128)(2,1)}) %all-gather.11.cloned.1.call-update) | async-done | bytes 4030480 | tf_op jit(solution)/shard_map/all_gather | solution.py:170
  219.8 11.1 %convert_reduce_fusion = (f32[768]{0:T(1024)}, bf16[8,328,768]{2,1,0:T(8,128)(2,1)S(1)}) fusion(f32[8,328,768]{2,1,0:T(8,128)} %get-tuple-element.173, f32[768]{0:T(1024)S(1)} %convert_element_type.398, bf16[768,768]{1,0:T(8,128)(2,1)} %param.48, bf16[1,8,328,768]{3,1,0,2:T(8,128)(2,1)} %all-gather.11.cloned.1.call-done), kind=kOutput, calls=%fused_computation.14 | convolution fusion | flops 3121593600 | bytes 17307648 | tf_op jit(solution)/shard_map/vfrd,kd->vfrk/dot_general | solution.py:172
  232.8 6.1 convert_bitcast_fusion
  239.6 26.3 %reduce-scatter.10.cloned.1.call-done = bf16[1,8,82,768]{3,1,2,0:T(8,128)(2,1)} async-done(((bf16[1,8,328,768]{3,1,2,0:T(8,128)(2,1)}), bf16[1,8,82,768]{3,1,2,0:T(8,128)(2,1)}) %reduce-scatter.10.cloned.1.call-update) | async-done | bytes 1007632 | tf_op jit(solution)/shard_map/reduce_scatter | solution.py:163
  265.8 45.9 %reduce-scatter.12.cloned.1.call-done = bf16[1,8,82,768]{3,1,2,0:T(8,128)(2,1)} async-done(((bf16[1,8,328,768]{3,1,2,0:T(8,128)(2,1)}), bf16[1,8,82,768]{3,1,2,0:T(8,128)(2,1)}) %reduce-scatter.12.cloned.1.call-update) | async-done | bytes 1007632 | tf_op jit(solution)/shard_map/reduce_scatter | solution.py:183
  323.4 31.2 %all-gather.13.cloned.1.call-done = bf16[1,8,328,768]{3,1,0,2:T(8,128)(2,1)} async-done(((bf16[1,8,82,768]{3,1,0,2:T(8,128)(2,1)}), bf16[1,8,328,768]{3,1,0,2:T(8,128)(2,1)}) %all-gather.13.cloned.1.call-update) | async-done | bytes 4030480 | tf_op jit(solution)/shard_map/all_gather | solution.py:188
  358.8 7.3 convert_reduce_fusion.1
  366.2 6.2 multiply_reduce_fusion
  372.4 6.5 multiply_convert_fusion
  387.1 9.4 %multiply_reduce_fusion.1 = (bf16[768]{0:T(1024)(128)(2,1)S(1)}, f32[8,329]{0,1:T(8,128)S(1)}, f32[8,329]{0,1:T(8,128)S(1)}) fusion(f32[8,329,768]{2,1,0:T(8,128)S(1)} %get-tuple-element.179, f32[8,329]{0,1:T(8,128)S(1)} %copy-done.22, f32[8,329]{0,1:T(8,128)S(1)} %copy-done.16, f32[8,1,768]{2,0,1:T(8,128)S(1)} %copy-done.32, ...), kind=kLoop, calls=%fused_computation.9 | loop fusion | flops 18186352 | bytes 16217728 | tf_op jit(solution)/shard_map/while/body/eval_jaxpr/reduce_sum | solution.py:229
  396.7 6.9 multiply_bitcast_fusion
  406.7 10.4 %psum.106 = f32[1,8,768]{2,1,0:T(8,128)S(1)} all-reduce(f32[1,8,768]{2,1,0:T(8,128)S(1)} %slice_bitcast_fusion), channel_id=1, replica_groups=mesh['videos'=8,'heads'=4] {'heads'}, use_global_device_ids=true, to_apply=%region_19.20 | all-reduce | flops 6144 | bytes 49152 | tf_op jit(solution)/shard_map/psum | solution.py:239
  420.3 5.7 slice.168
  432.4 10.8 %psum.107 = f32[1,8,768]{2,1,0:T(8,128)S(1)} all-reduce(f32[1,8,768]{2,1,0:T(8,128)} %convolution_bitcast_fusion.4), channel_id=1, replica_groups=mesh['videos'=8,'heads'=4] {'heads'}, use_global_device_ids=true, to_apply=%region_21.22 | all-reduce | flops 6144 | bytes 49152 | tf_op jit(solution)/shard_map/psum | solution.py:265
  449.9 9.0 %fusion.53 = f32[768,768]{1,0:T(8,128)} fusion(bf16[8,328,768]{2,1,0:T(8,128)(2,1)} %copy-done.83, bf16[8,328,768]{2,0,1:T(8,128)(2,1)} %bitcast.291), kind=kOutput, calls=%fused_computation.81 | convolution fusion | flops 3095396352 | bytes 10420224 | tf_op jit(solution)/shard_map/vfrd,vfrk->dk/dot_general | solution.py:176
  477.7 37.8 %all-reduce.1 = (f32[192]{0:T(256)}, f32[9,192]{1,0:T(8,128)S(1)}, f32[2,192]{1,0:T(2,128)}, f32[2,192]{1,0:T(2,128)}, f32[768]{0:T(1024)}) all-reduce(f32[192]{0:T(256)S(1)} %copy-done.68, bf16[9,192]{1,0:T(8,128)(2,1)S(1)} %copy.177, f32[2,192]{1,0:T(2,128)S(1)} %pad_maximum_fusion.4, ...), channel_id=1, replica_groups=mesh['videos'=8,'heads'=4] {'videos'}, use_global_device_ids=true, to_apply=%region_27.28 | all-reduce | flops 3456 | bytes 24192 | tf_op jit(solution)/shard_map/psum | solution.py:301
  518.8 320.8 %all-reduce.5.cloned.1.call-done = (f32[768,192]{0,1:T(8,128)}, f32[3,768,192]{1,2,0:T(8,128)}, f32[192,768]{1,0:T(8,128)}, f32[3,768,192]{1,2,0:T(8,128)}, f32[...) async-done(((f32[768,192]{0,1:T(8,128)}, f32[3,768,192]{1,2,0:T(8,128)}, f32[192,768]{1,0:T(8,128)}, f32[3,768,192]{1,2,0:T(8,128)}, f32[192,768]{1,0:T(8,128)}, ...) | async-done | bytes 10027024 | tf_op jit(solution)/shard_map/psum | solution.py:301
  (335 shorter events, 132.2 us)
Async XLA Ops:
  7.2 177.5 %copy-start = (bf16[768,768]{1,0:T(8,128)(2,1)S(1)}, bf16[768,768]{1,0:T(8,128)(2,1)}, u32[]{:S(2)}) copy-start(bf16[768,768]{1,0:T(8,128)(2,1)} %param.46) | copy-start | bytes 3538948
  7.2 38.7 %all-gather.7.cloned.1.call-start = ((), (), s32[]{:S(2)}) async-start(), calls=%async_computation.5 | async-start | bytes 5038080 | tf_op jit(solution)/shard_map/all_gather | solution.py:127
  7.9 137.9 %reduce-scatter.8.cloned.1.call-start = ((), (), s32[]{:S(2)}) async-start(), calls=%async_computation.6 | async-start | bytes 5038080 | tf_op jit(solution)/shard_map/reduce_scatter | solution.py:150
  10.6 45.6 %copy-start.47 = (f32[768]{0:T(1024)}, f32[768]{0:T(1024)S(1)}, u32[]{:S(2)}) copy-start(f32[768]{0:T(1024)S(1)} %convert_element_type.363) | copy-start | bytes 9220
  12.0 44.2 %copy-start.51 = (f32[768]{0:T(1024)}, f32[768]{0:T(1024)S(1)}, u32[]{:S(2)}) copy-start(f32[768]{0:T(1024)S(1)} %convert_element_type.364) | copy-start | bytes 9220
  52.5 18.7 %copy-start.33 = (f32[768,8]{0,1:T(8,128)}, f32[768,8]{0,1:T(8,128)S(1)}, u32[]{:S(2)}) copy-start(f32[768,8]{0,1:T(8,128)S(1)} %reshape.641) | copy-start | bytes 73732
  96.9 49.0 %copy-start.4 = (bf16[1,8,82,768]{3,1,2,0:T(8,128)(2,1)S(1)}, bf16[1,8,82,768]{3,1,2,0:T(8,128)(2,1)}, u32[]{:S(2)}) copy-start(bf16[1,8,82,768]{3,1,2,0:T(8,128)(2,1)} %param.26) | copy-start | bytes 3022852
  101.1 83.5 %all-gather.9.cloned.1.call-start = ((), (), s32[]{:S(2)}) async-start(), calls=%async_computation.7 | async-start | bytes 5038080 | tf_op jit(solution)/shard_map/all_gather | solution.py:157
  151.0 68.8 %all-gather.11.cloned.1.call-start = ((), (), s32[]{:S(2)}) async-start(), calls=%async_computation.9 | async-start | bytes 5038080 | tf_op jit(solution)/shard_map/all_gather | solution.py:170
  151.5 114.3 %reduce-scatter.10.cloned.1.call-start = ((), (), s32[]{:S(2)}) async-start(), calls=%async_computation.8 | async-start | bytes 5038080 | tf_op jit(solution)/shard_map/reduce_scatter | solution.py:163
  203.1 108.7 %reduce-scatter.12.cloned.1.call-start = ((), (), s32[]{:S(2)}) async-start(), calls=%async_computation.10 | async-start | bytes 5038080 | tf_op jit(solution)/shard_map/reduce_scatter | solution.py:183
  238.9 115.7 %all-gather.13.cloned.1.call-start = ((), (), s32[]{:S(2)}) async-start(), calls=%async_computation.11 | async-start | bytes 5038080 | tf_op jit(solution)/shard_map/all_gather | solution.py:188
  318.5 36.1 %copy-start.40 = (bf16[192,768]{1,0:T(8,128)(2,1)S(1)}, bf16[192,768]{1,0:T(8,128)(2,1)}, u32[]{:S(2)}) copy-start(bf16[192,768]{1,0:T(8,128)(2,1)} %param.42) | copy-start | bytes 884740
  320.9 155.9 %reduce-scatter.16.cloned.1.call-start = ((), (), s32[]{:S(2)}) async-start(), calls=%async_computation.13 | async-start | bytes 245760
  396.6 20.5 %copy-start.27 = (bf16[192,768]{1,0:T(8,128)(2,1)S(1)}, bf16[192,768]{1,0:T(8,128)(2,1)}, u32[]{:S(2)}) copy-start(bf16[192,768]{1,0:T(8,128)(2,1)} %param.36) | copy-start | bytes 884740
  396.6 20.7 %copy-start.46 = (f32[3,8,8]{1,2,0:T(8,128)S(1)}, f32[3,8,8]{1,2,0:T(8,128)}, u32[]{:S(2)}) copy-start(f32[3,8,8]{1,2,0:T(8,128)} %copy-done.45) | copy-start | bytes 2308
  396.6 20.7 %copy-start.57 = (bf16[8,3,64]{2,1,0:T(4,128)(2,1)S(1)}, bf16[8,3,64]{2,1,0:T(4,128)(2,1)}, u32[]{:S(2)}) copy-start(bf16[8,3,64]{2,1,0:T(4,128)(2,1)} %copy-done.56) | copy-start | bytes 9220
  396.6 22.2 %copy-start.59 = (bf16[8,3,64]{2,1,0:T(4,128)(2,1)S(1)}, bf16[8,3,64]{2,1,0:T(4,128)(2,1)}, u32[]{:S(2)}) copy-start(bf16[8,3,64]{2,1,0:T(4,128)(2,1)} %copy-done.58) | copy-start | bytes 9220
  396.7 22.3 %copy-start.64 = (bf16[8,3,64]{2,1,0:T(4,128)(2,1)S(1)}, bf16[8,3,64]{2,1,0:T(4,128)(2,1)}, u32[]{:S(2)}) copy-start(bf16[8,3,64]{2,1,0:T(4,128)(2,1)} %copy-done.63) | copy-start | bytes 9220
  420.3 22.9 %copy-start.48 = (f32[768]{0:T(1024)S(1)}, f32[768]{0:T(1024)}, u32[]{:S(2)}) copy-start(f32[768]{0:T(1024)} %copy-done.47) | copy-start | bytes 9220
  420.3 27.8 %copy-start.28 = (bf16[768,192]{0,1:T(8,128)(2,1)S(1)}, bf16[768,192]{0,1:T(8,128)(2,1)}, u32[]{:S(2)}) copy-start(bf16[768,192]{0,1:T(8,128)(2,1)} %param.30) | copy-start | bytes 884740
  446.6 69.5 %reduce-scatter.14.cloned.1.call-start = ((), (), s32[]{:S(2)}) async-start(), calls=%async_computation.12 | async-start | bytes 5038080 | tf_op jit(solution)/shard_map/reduce_scatter | solution.py:293
  449.6 390.0 %all-reduce.5.cloned.1.call-start = ((), (), s32[]{:S(2)}) async-start(), calls=%async_computation.14 | async-start | bytes 20054016 | tf_op jit(solution)/shard_map/psum | solution.py:301
  475.7 40.4 %copy-start.10 = (f32[1,8,82,768]{3,1,2,0:T(8,128)S(1)}, f32[1,8,82,768]{3,1,2,0:T(8,128)}, u32[]{:S(2)}) copy-start(f32[1,8,82,768]{3,1,2,0:T(8,128)} %copy-done.9) | copy-start | bytes 6045700
  (75 other events, 335.0 us)
Sparse Core Ops, SparseCore 0:
  9.6 36.2 all-gather.6
  101.3 44.5 reduce-scatter.7
  151.1 33.5 all-gather.8
  186.2 33.5 all-gather.10
  222.3 43.4 reduce-scatter.9
  268.2 43.4 reduce-scatter.11
  321.0 33.5 all-gather.12
  446.7 20.9 reduce-scatter.15
  470.5 43.4 reduce-scatter.13
  521.1 318.4 all-reduce.4
where the time goes:
time: 863 us; the launch traced here: 857 us
  waiting for transfers between devices  550 us (64%)
  matrix products  108 us (13%)
  blocking collectives  74.7 us (9%)
  other arithmetic  58.5 us (7%)
  local copies, waits for them, and re-layouts  47.4 us (5%)
  between operations  16.8 us (2%)
    psum x1, waiting for transfers between devices, on_device(): lax.psum((msg_fc_w_grad, msg_fc_b_grad, msg_qkv_w_grad, msg_qkv_b_grad, m...  321 us
    reduce_scatter x1, waiting for transfers between devices, on_device(): lax.psum_scatter(norm_two_part.astype(jnp.bfloat16), 'heads', scatter_dim...  45.9 us
    reduce_scatter x1, waiting for transfers between devices, on_device(): lax.psum_scatter(attn_part.astype(jnp.bfloat16), 'heads', scatter_dimensi...  44.1 us
    psum x1, blocking collectives, on_device(): lax.psum((msg_fc_w_grad, msg_fc_b_grad, msg_qkv_w_grad, msg_qkv_b_grad, m...  37.8 us
    all_gather x1, waiting for transfers between devices, on_device(): lax.all_gather(normed_two.astype(jnp.bfloat16), 'heads', axis=2, tiled=True)  33.1 us
    all_gather x1, waiting for transfers between devices, on_device(): gathered = lax.all_gather(frames, 'heads', axis=2, tiled=True)  31.4 us
    all_gather x1, waiting for transfers between devices, on_device(): grad_attn_full = lax.all_gather(grad_attn, 'heads', axis=2, tiled=True)  31.2 us
    unnamed x188, local copies, waits for them, and re-layouts  27.8 us
  transfers between devices with their start and end apart: 10, of which 8 were waited for; matrix products, arithmetic and copies ran while one was open for 9% of the time, Pallas kernels for 0%

commit v1 on v0

v1 whole, which is shorter than its diff:
```python
import jax
import jax.numpy as jnp
from jax import lax
from jax.sharding import PartitionSpec as P

HEAD_DIM = 64


epsilon = 1e-05


def norm_forward(value, gains, offset):
    average = jnp.mean(value, -1, keepdims=True)
    centered = value - average
    spread = jnp.mean(centered * centered, -1, keepdims=True)
    inverse = lax.rsqrt(spread + epsilon)
    unit = centered * inverse
    return (unit * gains.astype(jnp.float32) + offset.astype(jnp.float32), unit, inverse)


def norm_backward(gradient, unit, inverse, gains):
    scaled = gradient * gains.astype(jnp.float32)
    average = jnp.mean(scaled, -1, keepdims=True)
    second = jnp.mean(scaled * unit, -1, keepdims=True)
    return inverse * (scaled - average - unit * second)


def split_heads(tensors):
    return tuple(
        (
            tensor.reshape(tensor.shape[:-1] + (tensor.shape[-1] // HEAD_DIM, HEAD_DIM))
            for tensor in tensors
        )
    )


def project(normed, weight, biases):
    stacked = jnp.einsum("...d,cde->c...e", normed, weight, preferred_element_type=jnp.float32)
    return (
        (stacked[0] + biases[0]).astype(jnp.bfloat16),
        stacked[1].astype(jnp.bfloat16),
        (stacked[2] + biases[1]).astype(jnp.bfloat16),
    )


def attend_forward(queries, key_rows, values, keymask):
    scale_factor = HEAD_DIM ** (-0.5)
    scores = (
        jnp.einsum("bqhe,bkhe->bhqk", queries, key_rows, preferred_element_type=jnp.float32)
        * scale_factor
    )
    scores = jnp.where(keymask, scores, -1e30)
    largest = jnp.max(scores, -1, keepdims=True)
    exponent = jnp.exp(scores - largest)
    totals = jnp.sum(exponent, -1, keepdims=True)
    chances = exponent / totals
    output = jnp.einsum(
        "bhqk,bkhe->bqhe", chances.astype(jnp.bfloat16), values, preferred_element_type=jnp.float32
    )
    return (output.astype(jnp.bfloat16), largest + jnp.log(totals))


def attend_backward(queries, key_rows, values, keymask, log_total, grad_heads):
    scale_factor = HEAD_DIM ** (-0.5)
    scores = (
        jnp.einsum("bqhe,bkhe->bhqk", queries, key_rows, preferred_element_type=jnp.float32)
        * scale_factor
    )
    scores = jnp.where(keymask, scores, -1e30)
    chances = jnp.exp(scores - log_total)
    grad_chances = jnp.einsum(
        "bqhe,bkhe->bhqk", grad_heads, values, preferred_element_type=jnp.float32
    )
    deltas = jnp.sum(chances * grad_chances, -1, keepdims=True)
    grad_scores = (chances * (grad_chances - deltas)).astype(jnp.bfloat16)
    grad_query = (
        jnp.einsum("bhqk,bkhe->bqhe", grad_scores, key_rows, preferred_element_type=jnp.float32)
        * scale_factor
    ).astype(jnp.bfloat16)
    grad_key = (
        jnp.einsum("bhqk,bqhe->bkhe", grad_scores, queries, preferred_element_type=jnp.float32)
        * scale_factor
    ).astype(jnp.bfloat16)
    grad_value = jnp.einsum(
        "bhqk,bqhe->bkhe",
        chances.astype(jnp.bfloat16),
        grad_heads,
        preferred_element_type=jnp.float32,
    ).astype(jnp.bfloat16)
    return (grad_query, grad_key, grad_value)


def swap(value, axis, offset):
    size = lax.axis_size(axis)
    return lax.ppermute(value, axis, [(place, place ^ offset) for place in range(size)])


def pick(value, index, count):
    return lax.dynamic_slice_in_dim(value, index * count, count, 0)


def scatter_frames(frames, here, groups):
    slots, rows, features = frames.shape
    mine = slots // groups
    return [
        swap(pick(frames, here ^ offset, mine), "heads", offset)
        if offset
        else pick(frames, here, mine)
        for offset in range(groups)
    ]


def return_frames(value, here, groups, rows):
    mine, _, features = value.shape
    pieces = []
    for offset in range(groups):
        piece = value[:, offset * rows : (offset + 1) * rows]
        pieces.append(swap(piece, "heads", offset) if offset else piece)
    stacked = jnp.stack(pieces)
    order = jnp.arange(groups) ^ here
    return jnp.concatenate(
        [lax.dynamic_index_in_dim(stacked, here ^ place, 0, False) for place in range(groups)], 0
    )


def gather_blocks(block, groups):
    blocks = [block]
    offset = groups // 2
    found = {0: block}
    while offset:
        for known in list(found):
            found[known ^ offset] = swap(found[known], "heads", offset)
        offset //= 2
    return [found[place] for place in range(groups)]


def on_device(
    frames,
    out_grad,
    frame_tokens,
    frame_count,
    msg_fc_w,
    msg_fc_b,
    msg_norm_g,
    msg_norm_b,
    msg_qkv_w,
    msg_qkv_b,
    msg_out_w,
    msg_out_b,
    norm1_g,
    norm1_b,
    attn_qkv_w,
    attn_qkv_b,
    attn_out_w,
    attn_out_b,
    norm2_g,
    norm2_b,
    fc1_w,
    fc1_b,
    fc2_w,
    fc2_b,
):
    low = jnp.bfloat16
    full = jnp.float32
    _, slots, rows, features = frames.shape
    groups = lax.axis_size("heads")
    here = lax.axis_index("heads")
    mine = slots // groups
    all_rows = rows * groups
    padded = -(-(all_rows + 1) // 16) * 16
    width = msg_fc_w.shape[1]
    hidden_width = fc1_w.shape[1]
    frames = frames[0]
    out_grad = out_grad[0]

    row_blocks = scatter_frames(frames, here, groups)
    attn_pack = jnp.concatenate(
        [attn_qkv_w.transpose(0, 2, 1).reshape(3 * width, features), attn_out_w], 0
    )
    attn_packs = gather_blocks(attn_pack, groups)
    small_bias = jnp.concatenate([attn_qkv_b.reshape(-1), fc1_b])
    small_packs = lax.all_gather(small_bias, "heads")
    small_packs = [
        lax.dynamic_index_in_dim(small_packs, here ^ offset, 0, False) for offset in range(groups)
    ]
    fc_pack = jnp.stack([fc1_w, fc2_w])
    fc_packs = gather_blocks(fc_pack, groups)
    grad_blocks = scatter_frames(out_grad, here, groups)

    leading = lax.all_gather(frames[:, 0, :], "heads")[0]
    fc_part = jnp.dot(leading, msg_fc_w, preferred_element_type=full) + msg_fc_b
    message = lax.all_gather(fc_part, "heads", axis=1, tiled=True)
    msg_normed, msg_unit, msg_inverse = norm_forward(message, msg_norm_g, msg_norm_b)
    msg_in = msg_normed.astype(low)
    frame_mask = (jnp.arange(slots) < frame_count[0])[None, None, None, :]
    msg_query, msg_key, msg_value = split_heads(project(msg_in[None], msg_qkv_w, msg_qkv_b))
    msg_heads, msg_lse = attend_forward(msg_query, msg_key, msg_value, frame_mask)
    msg_flat = msg_heads.reshape(slots, width)
    msg_part = jnp.dot(msg_flat, msg_out_w, preferred_element_type=full)
    carried = message + jnp.sum(lax.all_gather(msg_part, "heads"), 0) + msg_out_b
    carried = pick(carried, here, mine)

    places = jnp.concatenate(
        [(here ^ offset) * rows + jnp.arange(rows) for offset in range(groups)]
    )
    tail = padded - all_rows
    row_mask = jnp.concatenate([places < frame_tokens[0], jnp.arange(tail) == 0])
    row_mask = row_mask[None, None, None, :]
    joined = jnp.concatenate(
        row_blocks
        + [carried[:, None, :].astype(low), jnp.zeros((mine, tail - 1, features), low)],
        1,
    ).astype(full)
    normed, unit, inverse = norm_forward(joined, norm1_g, norm1_b)
    normed = normed.astype(low)
    qkv_w = [
        jnp.concatenate([pack[part * width : (part + 1) * width] for pack in attn_packs], 0)
        for part in range(4)
    ]
    q_bias = jnp.concatenate([pack[:width] for pack in small_packs])
    v_bias = jnp.concatenate([pack[width : 2 * width] for pack in small_packs])
    fc1_bias = jnp.concatenate([pack[2 * width :] for pack in small_packs])

    def against(value, weight):
        return jnp.einsum("frd,ed->fre", value, weight, preferred_element_type=full)

    queries = (against(normed, qkv_w[0]) + q_bias).astype(low)
    key_rows = against(normed, qkv_w[1]).astype(low)
    values = (against(normed, qkv_w[2]) + v_bias).astype(low)
    queries, key_rows, values = split_heads((queries, key_rows, values))
    attn_heads, attn_lse = attend_forward(queries, key_rows, values, row_mask)
    attn_flat = attn_heads.reshape(mine, padded, features)
    attn_rows = attn_flat[:, :all_rows]
    mixed = (
        joined[:, :all_rows]
        + jnp.einsum("fre,ed->frd", attn_rows, qkv_w[3], preferred_element_type=full)
        + attn_out_b
    )

    normed_two, unit_two, inverse_two = norm_forward(mixed, norm2_g, norm2_b)
    mlp_in = normed_two.astype(low)
    fc1_full = jnp.concatenate([pack[0] for pack in fc_packs], 1)
    fc2_full = jnp.concatenate([pack[1] for pack in fc_packs], 0)
    hidden = jnp.einsum("frd,dk->frk", mlp_in, fc1_full, preferred_element_type=full) + fc1_bias
    gate = jax.nn.sigmoid(1.702 * hidden)
    active = (hidden * gate).astype(low)
    mixed_out = (
        mixed + jnp.einsum("frk,kd->frd", active, fc2_full, preferred_element_type=full) + fc2_b
    ).astype(low)
    mixed_out = return_frames(mixed_out, here, groups, rows)

    grad_low = jnp.concatenate(grad_blocks, 1)
    grad_top = grad_low.astype(full)
    grad_active = jnp.einsum("frd,kd->frk", grad_low, fc2_full, preferred_element_type=full)
    grad_hidden = (grad_active * (gate + 1.702 * hidden * gate * (1.0 - gate))).astype(low)
    grad_normed_two = jnp.einsum("frk,dk->frd", grad_hidden, fc1_full, preferred_element_type=full)
    grad_mixed = grad_top + norm_backward(grad_normed_two, unit_two, inverse_two, norm2_g)
    grad_attn = grad_mixed.astype(low)

    def by_block(value, axis):
        return jnp.split(value, groups, axis)

    active_blocks = by_block(active, 2)
    hidden_blocks = by_block(grad_hidden, 2)

    def fc_grads(block):
        return jnp.stack(
            [
                jnp.einsum("frd,frk->dk", mlp_in, hidden_blocks[block], preferred_element_type=full),
                jnp.einsum("frk,frd->kd", active_blocks[block], grad_low, preferred_element_type=full),
            ]
        ).astype(low)

    def collect(blocks):
        blocks = dict(enumerate(blocks))
        offset = 1
        while offset < groups:
            for place in [place for place in blocks if place & offset]:
                came = swap(blocks.pop(place), "heads", offset)
                kept = place ^ offset
                blocks[kept] = (blocks[kept].astype(full) + came.astype(full)).astype(low)
            offset *= 2
        return blocks[0]

    fc_total = collect([fc_grads(block) for block in range(groups)])
    fc_total = lax.psum(fc_total, "videos").astype(full)

    grad_o = jnp.einsum("frd,ed->fre", grad_attn, qkv_w[3], preferred_element_type=full).astype(low)
    grad_o = jnp.concatenate([grad_o, jnp.zeros((mine, tail, features), low)], 1)
    grad_query, grad_key, grad_value = attend_backward(
        queries, key_rows, values, row_mask, attn_lse, split_heads((grad_o,))[0]
    )
    parts = [part.reshape(mine, padded, features) for part in (grad_query, grad_key, grad_value)]
    grad_normed = sum(
        jnp.einsum("fre,ed->frd", part, weight, preferred_element_type=full)
        for part, weight in zip(parts, qkv_w)
    )
    grad_joined = norm_backward(grad_normed, unit, inverse, norm1_g)

    def total(value):
        return jnp.sum(value.astype(full), tuple(range(value.ndim - 1)))

    wide = [total(grad_hidden)]
    narrow = [
        total(grad_normed * unit),
        total(grad_normed),
        total(grad_attn),
        total(grad_normed_two * unit_two),
        total(grad_normed_two),
        total(grad_top),
    ]
    part_blocks = [by_block(part, 2) for part in parts]
    flat_blocks = by_block(attn_rows, 2)
    wide_blocks = by_block(wide[0], 0)
    q_sums = by_block(total(parts[0]), 0)
    v_sums = by_block(total(parts[2]), 0)
    narrow_all = jnp.stack([vector.reshape(groups, width) for vector in narrow], 1)

    def attn_grads(block):
        pieces = [
            jnp.einsum("fre,frd->ed", part[block], normed, preferred_element_type=full)
            for part in part_blocks
        ]
        pieces.append(
            jnp.einsum("fre,frd->ed", flat_blocks[block], grad_attn, preferred_element_type=full)
        )
        vectors = jnp.concatenate(
            [
                wide_blocks[block],
                q_sums[block],
                v_sums[block],
                lax.dynamic_index_in_dim(narrow_all, here ^ block, 0, False).reshape(-1),
            ]
        )
        count = vectors.shape[0]
        lines = -(-count // (16 * features)) * 16
        vectors = jnp.pad(vectors, (0, lines * features - count)).reshape(lines, features)
        return jnp.concatenate(pieces + [vectors], 0).astype(low)

    attn_total = collect([attn_grads(block) for block in range(groups)])
    attn_total = lax.psum(attn_total, "videos").astype(full)

    grad_carried = grad_joined[:, all_rows, :]
    grad_message = lax.all_gather(grad_carried, "heads", axis=0, tiled=True)
    grad_msg_low = grad_message.astype(low)
    msg_heads_grad = jnp.einsum("fd,ed->fe", grad_msg_low, msg_out_w, preferred_element_type=full)
    msg_gq, msg_gk, msg_gv = attend_backward(
        msg_query,
        msg_key,
        msg_value,
        frame_mask,
        msg_lse,
        split_heads((msg_heads_grad.astype(low)[None],))[0],
    )
    msg_stacked = jnp.stack([msg_gq, msg_gk, msg_gv]).reshape(3, slots, width)
    msg_norm_part = jnp.einsum("cfe,cde->fd", msg_stacked, msg_qkv_w, preferred_element_type=full)
    grad_msg_normed = jnp.sum(lax.all_gather(msg_norm_part, "heads"), 0)
    grad_fc = grad_message + norm_backward(grad_msg_normed, msg_unit, msg_inverse, msg_norm_g)
    grad_fc_cols = lax.dynamic_slice_in_dim(grad_fc, here * width, width, 1).astype(low)
    leading_part = jnp.einsum("fe,de->fd", grad_fc_cols, msg_fc_w, preferred_element_type=full)
    leading_grad = jnp.sum(lax.all_gather(leading_part, "heads"), 0)

    cut = lambda value: lax.dynamic_slice_in_dim(value, here * width, width, value.ndim - 1)
    operands = jnp.concatenate(
        [
            msg_in,
            msg_stacked[0],
            msg_stacked[1],
            msg_stacked[2],
            msg_flat,
            grad_msg_low,
            leading,
            grad_fc_cols,
        ],
        1,
    )
    operands = lax.all_gather(operands, "videos", axis=0, tiled=True)
    norm_sums = jnp.stack(
        [jnp.sum(cut(grad_msg_normed * msg_unit), 0), jnp.sum(cut(grad_msg_normed), 0)]
    )
    norm_sums = jnp.sum(lax.all_gather(norm_sums, "videos"), 0)
    marks = [0]
    for size in (features, width, width, width, width, features, features, width):
        marks.append(marks[-1] + size)
    all_in, all_q, all_k, all_v, all_flat, all_grad, all_lead, all_cols = [
        operands[:, begin:end] for begin, end in zip(marks[:-1], marks[1:])
    ]

    def outer(left, right):
        return jnp.einsum("rd,re->de", left, right, preferred_element_type=full)

    msg_qkv_w_grad = jnp.stack([outer(all_in, part) for part in (all_q, all_k, all_v)])
    msg_qkv_b_grad = jnp.stack([total(all_q), total(all_v)])
    msg_out_w_grad = outer(all_flat, all_grad)
    msg_out_b_grad = total(cut(all_grad))
    msg_fc_w_grad = outer(all_lead, all_cols)
    msg_fc_b_grad = total(all_cols)

    grad_frames = grad_mixed + grad_joined[:, :all_rows]
    frames_grad = return_frames(grad_frames.astype(low), here, groups, rows).astype(full)
    owner = (here == 0).astype(full)
    frames_grad = frames_grad.at[:, 0, :].add(leading_grad * owner)

    attn_w_total = attn_total[: 4 * width].reshape(4, width, features)
    sums = attn_total[4 * width :].reshape(-1)
    fc1_b_grad = sums[:hidden_width]
    sums = sums[hidden_width : hidden_width + 8 * width].reshape(8, width)
    return (
        mixed_out[None],
        frames_grad[None],
        msg_fc_w_grad,
        msg_fc_b_grad,
        norm_sums[0],
        norm_sums[1],
        msg_qkv_w_grad,
        msg_qkv_b_grad,
        msg_out_w_grad,
        msg_out_b_grad,
        sums[2],
        sums[3],
        attn_w_total[:3].transpose(0, 2, 1),
        sums[:2],
        attn_w_total[3],
        sums[4],
        sums[5],
        sums[6],
        fc_total[0],
        fc1_b_grad,
        fc_total[1],
        sums[7],
    )


def solution(mesh):
    placed = (
        P("videos", None, "heads", None),
        P("videos", None, "heads", None),
        P("videos"),
        P("videos"),
        P(None, "heads"),
        P("heads"),
        P(),
        P(),
        P(None, None, "heads"),
        P(None, "heads"),
        P("heads", None),
        P(),
        P(),
        P(),
        P(None, None, "heads"),
        P(None, "heads"),
        P("heads", None),
        P(),
        P(),
        P(),
        P(None, "heads"),
        P("heads"),
        P("heads", None),
        P(),
    )
    return jax.shard_map(
        on_device,
        mesh=mesh,
        in_specs=placed,
        out_specs=(
            P("videos", None, "heads", None),
            P("videos", None, "heads", None),
            P(None, "heads"),
            P("heads"),
            P("heads"),
            P("heads"),
            P(None, None, "heads"),
            P(None, "heads"),
            P("heads", None),
            P("heads"),
            P("heads"),
            P("heads"),
            P(None, None, "heads"),
            P(None, "heads"),
            P("heads", None),
            P("heads"),
            P("heads"),
            P("heads"),
            P(None, "heads"),
            P("heads"),
            P("heads", None),
            P("heads"),
        ),
        check_vma=False,
    )
```

time: 863 us -> 545 us (0.63)
  waiting for transfers between devices: 550 us -> 138 us
  blocking collectives: 74.7 us -> 132 us
  local copies, waits for them, and re-layouts: 47.4 us -> 71.3 us
  starting transfers between devices: 1.24 us -> 15.1 us
  other arithmetic: 58.5 us -> 45.3 us
  matrix products: 108 us -> 119 us
    psum x1, waiting for transfers between devices: 321 us -> 53 us  [on_device(): attn_total = lax.psum(attn_total, 'videos').astype(full)]
    all_gather x1 -> x9, blocking collectives: 5.26 us -> 132 us  [the longest x1 33.2 us: on_device(): operands = lax.all_gather(operands, 'videos', axis=0, tiled=True)]
    reduce_scatter x4 -> x0, waiting for transfers between devices: 116 us -> none  [the longest x1 45.9 us: on_device(): lax.psum_scatter(norm_two_part.astype(jnp.bfloat16), 'heads', scatter_dim...]
    all_gather x4 -> x0, waiting for transfers between devices: 112 us -> none  [the longest x1 33.1 us: on_device(): lax.all_gather(normed_two.astype(jnp.bfloat16), 'heads', axis=2, tiled=True)]
    ppermute x0 -> x24, waiting for transfers between devices: none -> 84.6 us  [swap(): lax.ppermute(value, axis, [(place, place ^ offset) for place in range(siz...]
    psum x4 -> x0, blocking collectives: 69.5 us -> none  [the longest x1 37.8 us: on_device(): lax.psum((msg_fc_w_grad, msg_fc_b_grad, msg_qkv_w_grad, msg_qkv_b_grad, m...]
    ppermute x0 -> x24, starting transfers between devices: none -> 15.1 us  [swap(): lax.ppermute(value, axis, [(place, place ^ offset) for place in range(siz...]
    dynamic_slice x0 -> x16, local copies, waits for them, and re-layouts: none -> 14.8 us  [the longest x10 12.4 us: pick(): return lax.dynamic_slice_in_dim(value, index * count, count, 0)]
  transfers between devices with their start and end apart: 10 -> 25, of which waited for: 8 -> 3; matrix products, arithmetic and copies ran while one was open for 9% -> 25% of each run, Pallas kernels for 0% -> 0%
where the time goes in v1:
time: 545 us; the launch traced here: 538 us
  waiting for transfers between devices  138 us (25%)
  blocking collectives  132 us (24%)
  matrix products  119 us (22%)
  local copies, waits for them, and re-layouts  71.3 us (13%)
  other arithmetic  45.3 us (8%)
  between operations  17.6 us (3%)
  starting transfers between devices  15.1 us (3%)
    ppermute x24, waiting for transfers between devices, swap(): lax.ppermute(value, axis, [(place, place ^ offset) for place in range(siz...  84.6 us
    psum x1, waiting for transfers between devices, on_device(): attn_total = lax.psum(attn_total, 'videos').astype(full)  53 us
    all_gather x1, blocking collectives, on_device(): operands = lax.all_gather(operands, 'videos', axis=0, tiled=True)  33.2 us
    all_gather x1, blocking collectives, on_device(): small_packs = lax.all_gather(small_bias, 'heads')  31.1 us
    all_gather x1, blocking collectives, on_device(): norm_sums = jnp.sum(lax.all_gather(norm_sums, 'videos'), 0)  27.4 us
    dot_general x1, matrix products, on_device(): jnp.einsum('frd,kd->frk', grad_low, fc2_full, preferred_element_type=full)  15.1 us
    ppermute x24, starting transfers between devices, swap(): lax.ppermute(value, axis, [(place, place ^ offset) for place in range(siz...  15.1 us
    dot_general x12, matrix products, attn_grads(): jnp.einsum('fre,frd->ed', part[block], normed, preferred_element_type=full)  14.9 us
  transfers between devices with their start and end apart: 25, of which 3 were waited for; matrix products, arithmetic and copies ran while one was open for 25% of the time, Pallas kernels for 0%

profile of v1, /device:TPU:0, one launch (start us, length us, event | category | flops | bytes accessed | tf_op | source)
XLA Modules:
  0.0 538.1 jit_solution(16468055941217280134)
XLA Ops:
  20.4 31.1 %all-gather.8 = bf16[4,1,1152]{2,1,0:T(2,128)(2,1)S(1)} all-gather(bf16[1,1,1152]{2,1,0:T(2,128)(2,1)S(1)} %reshape.648), channel_id=4, replica_groups=mesh['videos'=8,'heads'=4] {'heads'}, dimensions={0}, use_global_device_ids=true | all-gather | bytes 11520 | tf_op jit(solution)/shard_map/all_gather | solution.py:182
  52.8 5.2 all-gather
  58.1 5.3 all-gather.7
  66.7 5.3 all-gather.1
  87.3 8.2 %concatenate.137 = bf16[2,336,768]{2,1,0:T(8,128)(2,1)S(1)} concatenate(bf16[2,82,768]{2,1,0:T(8,128)(2,1)} %bitcast.458, bf16[2,82,768]{2,1,0:T(8,128)(2,1)} %collective-permute-done, bf16[2,82,768]{2,1,0:T(8,128)(2,1)} %collective-permute-done.1, bf16[2,82,768]{2,1,0:T(8,128)(2,1)} %collective-permute-done.2, bf16[2,1,768]{2,1,0:T(2,128)(2,1)S(1)} %copy.180, ...), dimensions={1} | concatenate | bytes 2064384 | tf_op jit(solution)/shard_map/concatenate | solution.py:209
  108.4 3.8 add_convert_fusion.7
  120.2 4.5 fusion.165
  126.8 12.7 %collective-permute-done.7 = bf16[2,768,768]{2,1,0:T(8,128)(2,1)} collective-permute-done((bf16[2,768,768]{2,1,0:T(8,128)(2,1)}, bf16[2,768,768]{2,1,0:T(8,128)(2,1)}, u32[]{:S(2)}, u32[]{:S(2)}) %collective-permute-start.7) | collective-permute-done | bytes 2359328 | tf_op jit(solution)/shard_map/ppermute | solution.py:95
  150.9 8.4 %multiply_convert_fusion.2 = (bf16[2,328,3072]{2,1,0:T(8,128)(2,1)}, f32[2,328,3072]{2,1,0:T(8,128)}) fusion(f32[3072]{0:T(1024)S(1)} %maximum_convert_fusion.1, bf16[2,328,768]{2,1,0:T(8,128)(2,1)S(1)} %add_convert_fusion.10, bf16[768,768]{1,0:T(8,128)(2,1)S(1)} %get-tuple-element.161, bf16[768,768]{1,0:T(8,128)(2,1)S(1)} %get-tuple-element.159, ...), kind=kOutput, calls=%fused_computation.9 | convolution fusion | flops 3128377344 | bytes 17829888 | tf_op jit(solution)/shard_map/frd,dk->frk/dot_general | solution.py:244
  159.4 15.1 %fusion.167 = (bf16[3072]{0:T(1024)(128)(2,1)S(1)}, bf16[2,328,3072]{2,1,0:T(8,128)(2,1)}) fusion(f32[2,328,3072]{2,1,0:T(8,128)} %get-tuple-element.241, f32[3072]{0:T(1024)S(1)} %maximum_convert_fusion.1, bf16[768,768]{1,0:T(8,128)(2,1)S(1)} %get-tuple-element.160, bf16[768,768]{1,0:T(8,128)(2,1)S(1)} %get-tuple-element.158, ...), kind=kOutput, calls=%fused_computation.387 | convolution fusion | flops 3142480896 | bytes 17836032 | tf_op jit(solution)/shard_map/frd,kd->frk/dot_general | solution.py:254
  174.5 6.1 %multiply_reduce_fusion.4 = (bf16[768]{0:T(1024)(128)(2,1)S(1)}, f32[2,328]{1,0:T(2,128)S(1)}, f32[2,328]{1,0:T(2,128)S(1)}, bf16[768]{0:T(1024)(128)(2,1)S(1)}, f32[2,328,768]{2,1,0:T(8,128)S(1)}) fusion(f32[2,328,768]{2,1,0:T(8,128)S(1)} %get-tuple-element.239, f32[2,328]{1,0:T(2,128)S(1)} %add_rsqrt_fusion, f32[2,328]{1,0:T(2,128)S(1)} %broadcast_multiply_fusion.4, ...), kind=kOutput, calls=%fused_computation.51 | convolution fusion | flops 3118801920 | bytes 12796160 | tf_op jit(solution)/shard_map/frk,dk->frd/dot_general | solution.py:256
  193.9 7.8 %bitcast_reduce_fusion = (bf16[12,64]{1,0:T(8,128)(2,1)S(1)}, bf16[2,12,64,336]{3,2,1,0:T(8,128)(2,1)}) fusion(bf16[2,336,12,64]{1,3,2,0:T(8,128)(2,1)S(1)} %bitcast.423, f32[2,12,336,336]{2,3,1,0:T(8,128)} %copy-done.1, f32[2,12,336]{2,1,0:T(8,128)S(1)} %log_add_fusion), kind=kOutput, calls=%fused_computation.141 | convolution fusion | flops 353266944 | bytes 12936192 | tf_op jit(solution)/shard_map/bhqk,bqhe->bkhe/dot_general | solution.py:84
  201.7 8.8 %multiply_reduce_fusion = (f32[2,12,336]{2,1,0:T(8,128)S(1)}, f32[2,12,336,336]{2,3,1,0:T(8,128)}) fusion(f32[2,12,336,336]{2,3,1,0:T(8,128)} %copy-done.1, f32[2,12,336]{2,1,0:T(8,128)S(1)} %log_add_fusion, bf16[2,336,12,64]{1,3,2,0:T(8,128)(2,1)S(1)} %bitcast.424, bf16[2,336,12,64]{1,3,2,0:T(8,128)(2,1)S(1)} %bitcast.426), kind=kOutput, calls=%fused_computation.1 | convolution fusion | flops 354936960 | bytes 23804928 | tf_op jit(solution)/shard_map/bqhe,bkhe->bhqk/dot_general | solution.py:71
  210.5 6.8 %multiply_convert_fusion = bf16[2,12,336,336]{2,3,1,0:T(8,128)(2,1)S(1)} fusion(f32[2,12,336,336]{2,3,1,0:T(8,128)} %get-tuple-element.244, f32[2,12,336,336]{2,3,1,0:T(8,128)S(1)} %bitcast.418, f32[2,12,336]{2,1,0:T(8,128)S(1)} %get-tuple-element.243, f32[2,12,336]{2,1,0:T(8,128)S(1)} %log_add_fusion), kind=kLoop, calls=%fused_computation | loop fusion | flops 10838016 | bytes 27159552 | tf_op jit(solution)/shard_map/convert_element_type | solution.py:75
  228.2 5.5 %all-gather.3 = f32[8,1,768]{2,1,0:T(1,128)S(1)} all-gather(f32[2,1,768]{2,1,0:T(1,128)S(1)} %slice.441), channel_id=5, replica_groups=mesh['videos'=8,'heads'=4] {'heads'}, dimensions={0}, use_global_device_ids=true | all-gather | bytes 30720 | tf_op jit(solution)/shard_map/all_gather | solution.py:344
  240.5 6.8 %add_convert_fusion.9 = bf16[2,328,768]{2,1,0:T(8,128)(2,1)S(1)} fusion(f32[2,328,768]{2,1,0:T(8,128)S(1)} %get-tuple-element.239, bf16[2,328,3072]{2,1,0:T(8,128)(2,1)} %get-tuple-element.240, bf16[768,768]{1,0:T(8,128)(2,1)} %copy-done.33, bf16[768,768]{1,0:T(8,128)(2,1)} %copy-done.30, bf16[768,768]{1,0:T(8,128)(2,1)} %copy-done.31, ...), kind=kOutput, calls=%fused_computation.54 | convolution fusion | flops 3115782144 | bytes 11774976 | tf_op jit(solution)/shard_map/frk,kd->frd/dot_general | solution.py:248
  259.7 3.8 convert_reduce_fusion
  264.9 5.7 %all-gather.4 = f32[32,768]{1,0:T(8,128)S(1)} all-gather(f32[8,768]{1,0:T(8,128)S(1)} %convolution_bitcast_fusion.19), channel_id=6, replica_groups=mesh['videos'=8,'heads'=4] {'heads'}, dimensions={0}, use_global_device_ids=true | all-gather | bytes 122880 | tf_op jit(solution)/shard_map/all_gather | solution.py:357
  298.6 71.8 %collective-permute-done.20 = bf16[784,768]{1,0:T(8,128)(2,1)S(1)} collective-permute-done((bf16[784,768]{1,0:T(8,128)(2,1)S(1)}, bf16[784,768]{1,0:T(8,128)(2,1)S(1)}, u32[]{:S(2)}, u32[]{:S(2)}) %collective-permute-start.20) | collective-permute-done | bytes 1204256 | tf_op jit(solution)/shard_map/ppermute | solution.py:95
  371.9 4.0 add_convert_fusion
  376.7 27.4 %all-gather.9 = f32[8,2,192]{2,1,0:T(2,128)S(1)} all-gather(f32[1,2,192]{2,1,0:T(2,128)S(1)} %maximum_bitcast_fusion.21), channel_id=8, replica_groups=mesh['videos'=8,'heads'=4] {'videos'}, dimensions={0}, use_global_device_ids=true | all-gather | bytes 13824 | tf_op jit(solution)/shard_map/all_gather | solution.py:381
  404.2 33.2 %all_gather.53 = bf16[64,3264]{1,0:T(8,128)(2,1)S(1)} all-gather(bf16[8,3264]{1,0:T(8,128)(2,1)S(1)} %concatenate.168), channel_id=1, replica_groups=mesh['videos'=8,'heads'=4] {'videos'}, dimensions={0}, use_global_device_ids=true | all-gather | bytes 470016 | tf_op jit(solution)/shard_map/all_gather | solution.py:377
  439.0 13.2 %all-gather.5 = f32[32,768]{1,0:T(8,128)S(1)} all-gather(f32[8,768]{1,0:T(8,128)S(1)} %fusion.169), channel_id=7, replica_groups=mesh['videos'=8,'heads'=4] {'heads'}, dimensions={0}, use_global_device_ids=true | all-gather | bytes 122880 | tf_op jit(solution)/shard_map/all_gather | solution.py:361
  468.1 53.0 %all-reduce.8.cloned.1.call-done = (bf16[784,768]{1,0:T(8,128)(2,1)}, bf16[2,768,768]{2,1,0:T(8,128)(2,1)}) async-done(((bf16[784,768]{1,0:T(8,128)(2,1)}, bf16[2,768,768]{2,1,0:T(8,128)(2,1)}), (bf16[784,768]{1,0:T(8,128)(2,1)}, bf16[2,768,768]{2,1,0:T(8,128)(2,1)})) %all-reduce.8.cloned.1.call-update) | async-done | bytes 3563536 | tf_op jit(solution)/shard_map/psum | solution.py:341
  (502 shorter events, 167.0 us)
Async XLA Ops:
  7.2 513.9 %all-reduce.8.cloned.1.call-start = ((), (), s32[]{:S(2)}) async-start(), calls=%async_computation | async-start | bytes 7127040 | tf_op jit(solution)/shard_map/psum | solution.py:341
  9.7 85.8 %collective-permute-start.4 = (bf16[768,768]{1,0:T(8,128)(2,1)}, bf16[768,768]{1,0:T(8,128)(2,1)S(1)}, u32[]{:S(2)}, u32[]{:S(2)}) collective-permute-start(bf16[768,768]{1,0:T(8,128)(2,1)} %pad_maximum_fusion.4), channel_id=1, source_target_pairs={{0,2},{1,3},{2,0},{3,1},{4,6},{5,7},{6,4},{7,5},{8,10},{9,11},{10,... | collective-permute-start | bytes 3538952 | tf_op jit(solution)/shard_map/ppermute | solution.py:95
  12.7 86.0 %collective-permute-start.3 = (bf16[768,768]{1,0:T(8,128)(2,1)}, bf16[768,768]{1,0:T(8,128)(2,1)}, u32[]{:S(2)}, u32[]{:S(2)}) collective-permute-start(bf16[768,768]{1,0:T(8,128)(2,1)} %pad_maximum_fusion.4), channel_id=1, source_target_pairs={{0,1},{1,0},{2,3},{3,2},{4,5},{5,4},{6,7},{7,6},{8,9},{9,8},{10,11... | collective-permute-start | bytes 3538952 | tf_op jit(solution)/shard_map/ppermute | solution.py:95
  17.0 68.1 %collective-permute-start = (bf16[2,82,768]{2,1,0:T(8,128)(2,1)}, bf16[2,82,768]{2,1,0:T(8,128)(2,1)}, u32[]{:S(2)}, u32[]{:S(2)}) collective-permute-start(bf16[2,82,768]{2,1,0:T(8,128)(2,1)} %bitcast.407), channel_id=1, source_target_pairs={{0,1},{1,0},{2,3},{3,2},{4,5},{5,4},{6,7},{7,6},{8,9},{9,8},{10,11... | collective-permute-start | bytes 755720 | tf_op jit(solution)/shard_map/ppermute | solution.py:95
  18.2 68.6 %collective-permute-start.1 = (bf16[2,82,768]{2,1,0:T(8,128)(2,1)}, bf16[2,82,768]{2,1,0:T(8,128)(2,1)}, u32[]{:S(2)}, u32[]{:S(2)}) collective-permute-start(bf16[2,82,768]{2,1,0:T(8,128)(2,1)} %bitcast.406), channel_id=1, source_target_pairs={{0,2},{1,3},{2,0},{3,1},{4,6},{5,7},{6,4},{7,5},{8,10},{9,11},{10,... | collective-permute-start | bytes 755720 | tf_op jit(solution)/shard_map/ppermute | solution.py:95
  19.0 67.9 %collective-permute-start.2 = (bf16[2,82,768]{2,1,0:T(8,128)(2,1)}, bf16[2,82,768]{2,1,0:T(8,128)(2,1)}, u32[]{:S(2)}, u32[]{:S(2)}) collective-permute-start(bf16[2,82,768]{2,1,0:T(8,128)(2,1)} %bitcast.405), channel_id=1, source_target_pairs={{0,3},{1,2},{2,1},{3,0},{4,7},{5,6},{6,5},{7,4},{8,11},{9,10},{10,... | collective-permute-start | bytes 755720 | tf_op jit(solution)/shard_map/ppermute | solution.py:95
  85.0 54.4 %collective-permute-start.7 = (bf16[2,768,768]{2,1,0:T(8,128)(2,1)}, bf16[2,768,768]{2,1,0:T(8,128)(2,1)}, u32[]{:S(2)}, u32[]{:S(2)}) collective-permute-start(bf16[2,768,768]{2,1,0:T(8,128)(2,1)} %pad_maximum_fusion), channel_id=1, source_target_pairs={{0,2},{1,3},{2,0},{3,1},{4,6},{5,7},{6,4},{7,5},{8,10},{9,11},{10,... | collective-permute-start | bytes 7077896 | tf_op jit(solution)/shard_map/ppermute | solution.py:95
  86.8 59.7 %collective-permute-start.6 = (bf16[2,768,768]{2,1,0:T(8,128)(2,1)}, bf16[2,768,768]{2,1,0:T(8,128)(2,1)}, u32[]{:S(2)}, u32[]{:S(2)}) collective-permute-start(bf16[2,768,768]{2,1,0:T(8,128)(2,1)} %pad_maximum_fusion), channel_id=1, source_target_pairs={{0,1},{1,0},{2,3},{3,2},{4,5},{5,4},{6,7},{7,6},{8,9},{9,8},{10,11... | collective-permute-start | bytes 7077896 | tf_op jit(solution)/shard_map/ppermute | solution.py:95
  86.9 72.4 %collective-permute-start.13 = (bf16[2,82,768]{2,1,0:T(8,128)(2,1)}, bf16[2,82,768]{2,1,0:T(8,128)(2,1)}, u32[]{:S(2)}, u32[]{:S(2)}) collective-permute-start(bf16[2,82,768]{2,1,0:T(8,128)(2,1)} %bitcast.402), channel_id=1, source_target_pairs={{0,2},{1,3},{2,0},{3,1},{4,6},{5,7},{6,4},{7,5},{8,10},{9,11},{10,... | collective-permute-start | bytes 755720 | tf_op jit(solution)/shard_map/ppermute | solution.py:95
  95.5 7.1 %collective-permute-start.5 = (bf16[768,768]{1,0:T(8,128)(2,1)S(1)}, bf16[768,768]{1,0:T(8,128)(2,1)S(1)}, u32[]{:S(2)}, u32[]{:S(2)}) collective-permute-start(bf16[768,768]{1,0:T(8,128)(2,1)S(1)} %collective-permute-done.4), channel_id=1, source_target_pairs={{0,1},{1,0},{2,3},{3,2},{4,5},{5,4},{6,7},{7,6},{8,9},{9,8},{10,11... | collective-permute-start | bytes 3538952 | tf_op jit(solution)/shard_map/ppermute | solution.py:95
  98.8 60.6 %collective-permute-start.14 = (bf16[2,82,768]{2,1,0:T(8,128)(2,1)}, bf16[2,82,768]{2,1,0:T(8,128)(2,1)}, u32[]{:S(2)}, u32[]{:S(2)}) collective-permute-start(bf16[2,82,768]{2,1,0:T(8,128)(2,1)} %bitcast.401), channel_id=1, source_target_pairs={{0,3},{1,2},{2,1},{3,0},{4,7},{5,6},{6,5},{7,4},{8,11},{9,10},{10,... | collective-permute-start | bytes 755720 | tf_op jit(solution)/shard_map/ppermute | solution.py:95
  102.7 56.7 %collective-permute-start.12 = (bf16[2,82,768]{2,1,0:T(8,128)(2,1)}, bf16[2,82,768]{2,1,0:T(8,128)(2,1)}, u32[]{:S(2)}, u32[]{:S(2)}) collective-permute-start(bf16[2,82,768]{2,1,0:T(8,128)(2,1)} %bitcast.403), channel_id=1, source_target_pairs={{0,1},{1,0},{2,3},{3,2},{4,5},{5,4},{6,7},{7,6},{8,9},{9,8},{10,11... | collective-permute-start | bytes 755720 | tf_op jit(solution)/shard_map/ppermute | solution.py:95
  139.5 9.3 %collective-permute-start.8 = (bf16[2,768,768]{2,1,0:T(8,128)(2,1)}, bf16[2,768,768]{2,1,0:T(8,128)(2,1)S(1)}, u32[]{:S(2)}, u32[]{:S(2)}) collective-permute-start(bf16[2,768,768]{2,1,0:T(8,128)(2,1)} %collective-permute-done.7), channel_id=1, source_target_pairs={{0,1},{1,0},{2,3},{3,2},{4,5},{5,4},{6,7},{7,6},{8,9},{9,8},{10,11... | collective-permute-start | bytes 7077896 | tf_op jit(solution)/shard_map/ppermute | solution.py:95
  248.3 209.5 %collective-permute-start.11 = (bf16[2,82,768]{2,1,0:T(8,128)(2,1)}, bf16[2,82,768]{2,1,0:T(8,128)(2,1)}, u32[]{:S(2)}, u32[]{:S(2)}) collective-permute-start(bf16[2,82,768]{2,1,0:T(8,128)(2,1)} %get-tuple-element.193), channel_id=1, source_target_pairs={{0,3},{1,2},{2,1},{3,0},{4,7},{5,6},{6,5},{7,4},{8,11},{9,10},{10,... | collective-permute-start | bytes 755720 | tf_op jit(solution)/shard_map/ppermute | solution.py:95
  254.5 117.4 %collective-permute-start.21 = (bf16[2,768,768]{2,1,0:T(8,128)(2,1)}, bf16[2,768,768]{2,1,0:T(8,128)(2,1)}, u32[]{:S(2)}, u32[]{:S(2)}) collective-permute-start(bf16[2,768,768]{2,1,0:T(8,128)(2,1)} %pad_maximum_fusion.1), channel_id=1, source_target_pairs={{0,1},{1,0},{2,3},{3,2},{4,5},{5,4},{6,7},{7,6},{8,9},{9,8},{10,11... | collective-permute-start | bytes 7077896 | tf_op jit(solution)/shard_map/ppermute | solution.py:95
  259.0 29.1 %collective-permute-start.22 = (bf16[2,768,768]{2,1,0:T(8,128)(2,1)}, bf16[2,768,768]{2,1,0:T(8,128)(2,1)}, u32[]{:S(2)}, u32[]{:S(2)}) collective-permute-start(bf16[2,768,768]{2,1,0:T(8,128)(2,1)} %pad_maximum_fusion.2), channel_id=1, source_target_pairs={{0,1},{1,0},{2,3},{3,2},{4,5},{5,4},{6,7},{7,6},{8,9},{9,8},{10,11... | collective-permute-start | bytes 7077896 | tf_op jit(solution)/shard_map/ppermute | solution.py:95
  277.9 20.2 %collective-permute-start.18 = (bf16[784,768]{1,0:T(8,128)(2,1)S(1)}, bf16[784,768]{1,0:T(8,128)(2,1)S(1)}, u32[]{:S(2)}, u32[]{:S(2)}) collective-permute-start(bf16[784,768]{1,0:T(8,128)(2,1)S(1)} %constant_dynamic-update-slice_fusion.1), channel_id=1, source_target_pairs={{0,1},{1,0},{2,3},{3,2},{4,5},{5,4},{6,7},{7,6},{8,9},{9,8},{10,11... | collective-permute-start | bytes 3612680 | tf_op jit(solution)/shard_map/ppermute | solution.py:95
  278.3 13.8 %collective-permute-start.19 = (bf16[784,768]{1,0:T(8,128)(2,1)S(1)}, bf16[784,768]{1,0:T(8,128)(2,1)S(1)}, u32[]{:S(2)}, u32[]{:S(2)}) collective-permute-start(bf16[784,768]{1,0:T(8,128)(2,1)S(1)} %constant_dynamic-update-slice_fusion.3), channel_id=1, source_target_pairs={{0,1},{1,0},{2,3},{3,2},{4,5},{5,4},{6,7},{7,6},{8,9},{9,8},{10,11... | collective-permute-start | bytes 3612680 | tf_op jit(solution)/shard_map/ppermute | solution.py:95
  290.4 81.5 %collective-permute-start.23 = (bf16[2,768,768]{2,1,0:T(8,128)(2,1)S(1)}, bf16[2,768,768]{2,1,0:T(8,128)(2,1)S(1)}, u32[]{:S(2)}, u32[]{:S(2)}) collective-permute-start(bf16[2,768,768]{2,1,0:T(8,128)(2,1)S(1)} %add_convert_fusion.1), channel_id=1, source_target_pairs={{0,2},{1,3},{2,0},{3,1},{4,6},{5,7},{6,4},{7,5},{8,10},{9,11},{10,... | collective-permute-start | bytes 7077896 | tf_op jit(solution)/shard_map/ppermute | solution.py:95
  292.5 77.9 %collective-permute-start.20 = (bf16[784,768]{1,0:T(8,128)(2,1)S(1)}, bf16[784,768]{1,0:T(8,128)(2,1)S(1)}, u32[]{:S(2)}, u32[]{:S(2)}) collective-permute-start(bf16[784,768]{1,0:T(8,128)(2,1)S(1)} %add_convert_fusion.4), channel_id=1, source_target_pairs={{0,2},{1,3},{2,0},{3,1},{4,6},{5,7},{6,4},{7,5},{8,10},{9,11},{10,... | collective-permute-start | bytes 3612680 | tf_op jit(solution)/shard_map/ppermute | solution.py:95
  298.1 160.6 %collective-permute-start.10 = (bf16[2,82,768]{2,1,0:T(8,128)(2,1)S(1)}, bf16[2,82,768]{2,1,0:T(8,128)(2,1)S(1)}, u32[]{:S(2)}, u32[]{:S(2)}) collective-permute-start(bf16[2,82,768]{2,1,0:T(8,128)(2,1)S(1)} %copy-done.68), channel_id=1, source_target_pairs={{0,2},{1,3},{2,0},{3,1},{4,6},{5,7},{6,4},{7,5},{8,10},{9,11},{10,... | collective-permute-start | bytes 755720 | tf_op jit(solution)/shard_map/ppermute | solution.py:95
  370.4 88.3 %collective-permute-start.9 = (bf16[2,82,768]{2,1,0:T(8,128)(2,1)S(1)}, bf16[2,82,768]{2,1,0:T(8,128)(2,1)S(1)}, u32[]{:S(2)}, u32[]{:S(2)}) collective-permute-start(bf16[2,82,768]{2,1,0:T(8,128)(2,1)S(1)} %copy-done.67), channel_id=1, source_target_pairs={{0,1},{1,0},{2,3},{3,2},{4,5},{5,4},{6,7},{7,6},{8,9},{9,8},{10,11... | collective-permute-start | bytes 755720 | tf_op jit(solution)/shard_map/ppermute | solution.py:95
  437.6 22.1 %collective-permute-start.17 = (bf16[2,82,768]{2,1,0:T(8,128)(2,1)S(1)}, bf16[2,82,768]{2,1,0:T(8,128)(2,1)S(1)}, u32[]{:S(2)}, u32[]{:S(2)}) collective-permute-start(bf16[2,82,768]{2,1,0:T(8,128)(2,1)S(1)} %get-tuple-element.185), channel_id=1, source_target_pairs={{0,3},{1,2},{2,1},{3,0},{4,7},{5,6},{6,5},{7,4},{8,11},{9,10},{10,... | collective-permute-start | bytes 755720 | tf_op jit(solution)/shard_map/ppermute | solution.py:95
  437.7 22.1 %collective-permute-start.16 = (bf16[2,82,768]{2,1,0:T(8,128)(2,1)S(1)}, bf16[2,82,768]{2,1,0:T(8,128)(2,1)S(1)}, u32[]{:S(2)}, u32[]{:S(2)}) collective-permute-start(bf16[2,82,768]{2,1,0:T(8,128)(2,1)S(1)} %get-tuple-element.186), channel_id=1, source_target_pairs={{0,2},{1,3},{2,0},{3,1},{4,6},{5,7},{6,4},{7,5},{8,10},{9,11},{10,... | collective-permute-start | bytes 755720 | tf_op jit(solution)/shard_map/ppermute | solution.py:95
  (103 other events, 1065.9 us)
Sparse Core Ops, SparseCore 0:
  376.1 144.9 all-reduce.7
